TPU v7x, 128 devices: a whole 4x4x4 slice. The times are simulated.
128 devices in a mesh: dp: 64 (over z, x_hi, y, core), tensor: 2 (over x_lo).
Axes of the slice: x: 4 (x_hi: 2, x_lo: 2; x = x_hi * 2 + x_lo), y: 4, z: 4, core: 2. Of those that a mesh axis runs over, the one named last changes fastest.
Arguments:
- resid: bfloat16 [32768, 1536], P(('dp', 'tensor')), may hold values from -6 to 6
- cotangent: bfloat16 [32768, 1536], P(('dp', 'tensor')), may hold values from -6 to 6
- segments: int32 [32768], P('dp'), may hold values from 0 to 127, as said below
- pre_gain: bfloat16 [1536], P(('dp', 'tensor')), may hold values from 0.25 to 1.75
- w_z: bfloat16 [1536, 3072], P('dp', 'tensor'), may hold values from -0.15625 to 0.15625
- w_x: bfloat16 [1536, 3072], P('dp', 'tensor'), may hold values from -0.5 to 0.5
- w_bc: bfloat16 [1536, 256], P(('dp', 'tensor')), may hold values from -0.15625 to 0.15625
- w_dt: bfloat16 [1536, 48], P('dp', 'tensor'), may hold values from -0.15625 to 0.15625
- conv_x: float32 [4, 3072], P(None, 'tensor'), may hold values from -3 to 3
- conv_x_bias: float32 [3072], P('tensor'), may hold values from -3 to 3
- conv_bc: float32 [4, 256], replicated, may hold values from -3 to 3
- conv_bc_bias: float32 [256], replicated, may hold values from -3 to 3
- dt_bias: float32 [48], P('tensor'), may hold values from -1 to 0.5
- a_log: float32 [48], P('tensor'), may hold values from -6.9 to -3
- d_skip: float32 [48], P('tensor'), may hold values from 0.5 to 1.5
- gate_gain: float32 [3072], P('tensor'), may hold values from 0.25 to 1.75
- w_out: bfloat16 [3072, 1536], P('tensor', 'dp'), may hold values from -0.109375 to 0.109375
Outputs:
- out: bfloat16 [32768, 1536], P(('dp', 'tensor'))
- grad_resid: float32 [32768, 1536], P(('dp', 'tensor'))
- grad_pre_gain: float32 [1536], P(('dp', 'tensor'))
- grad_w_z: float32 [1536, 3072], P('dp', 'tensor')
- grad_w_x: float32 [1536, 3072], P('dp', 'tensor')
- grad_w_bc: float32 [1536, 256], P(('dp', 'tensor'))
- grad_w_dt: float32 [1536, 48], P('dp', 'tensor')
- grad_conv_x: float32 [4, 3072], P(None, 'tensor')
- grad_conv_x_bias: float32 [3072], P('tensor')
- grad_conv_bc: float32 [4, 256], replicated
- grad_conv_bc_bias: float32 [256], replicated
- grad_dt_bias: float32 [48], P('tensor')
- grad_a_log: float32 [48], P('tensor')
- grad_d_skip: float32 [48], P('tensor')
- grad_gate_gain: float32 [3072], P('tensor')
- grad_w_out: float32 [3072, 1536], P('tensor', 'dp')
Inputs may be any that keep to these rules, and one draw needn't show every extreme that they name: `segments`: numbers never fall along the tokens; each sequence of 512 tokens holds exactly two documents, the first of sequence s numbered 2 s and the second 2 s + 1, each of one token or more.
All inputs are finite; a program needn't handle non-finite values.
Results may differ from a plain program's by a relative error of at most 0.011.
Values may be sent and summed in bfloat16 or wider, within the bound.
No kernel may reach another device: no remote copies, remote signals or barrier semaphores. Data moves between devices by JAX's collectives and lax.ppermute only.
A program may use at most 192 MiB of HBM per device.

v0:
```python
import jax
import jax.numpy as jnp
from jax import lax
from jax.sharding import PartitionSpec as P

GROUP = 256


EPS = 1e-05
HIGH = lax.Precision.HIGHEST


def silu_act(values):
    return values * jax.nn.sigmoid(values)


def conv_mix(values, kernel, conv_bias, segment):
    kernel_size = kernel.shape[0]
    row_count = values.shape[0]
    padded = jnp.concatenate(
        [jnp.zeros((kernel_size - 1, values.shape[1]), values.dtype), values], axis=0
    )
    seg_pad = jnp.concatenate([jnp.full((kernel_size - 1,), -1, jnp.int32), segment], axis=0)
    summed = jnp.broadcast_to(conv_bias[None, :], values.shape)
    for offset in range(kernel_size):
        window = padded[offset : offset + row_count]
        keep_mask = (seg_pad[offset : offset + row_count] == segment).astype(values.dtype)
        summed = summed + window * kernel[offset][None, :] * keep_mask[:, None]
    return summed


def ssd_scan(x_heads, dt_full, decay_rate, b_state, c_state, segment):
    length = x_heads.shape[0]
    head_count = x_heads.shape[1]
    head_size = x_heads.shape[2]
    nstate = b_state.shape[1]
    blocks = length // GROUP
    row_ids = lax.broadcasted_iota(jnp.int32, (GROUP, GROUP), 0)
    col_ids = lax.broadcasted_iota(jnp.int32, (GROUP, GROUP), 1)
    causal = row_ids >= col_ids

    def regroup(values):
        return values.reshape((blocks, GROUP) + values.shape[1:])

    def advance(carried, pieces):
        states, last_seg = carried
        x_blk, dt_blk, b_blk, c_blk, seg_blk = pieces
        log_decay = jnp.cumsum(dt_blk * decay_rate[None, :], axis=0).T
        log_gaps = log_decay[:, :, None] - log_decay[:, None, :]
        inside = causal & (seg_blk[:, None] == seg_blk[None, :])
        decays = jnp.where(inside[None], jnp.exp(jnp.minimum(log_gaps, 0.0)), 0.0)
        scores = jnp.einsum("in,jn->ij", c_blk, b_blk, precision=HIGH)
        mixing = decays * scores[None] * dt_blk.T[:, None, :]
        within = jnp.einsum("hij,jhp->ihp", mixing, x_blk, precision=HIGH)
        alive_mask = (seg_blk == last_seg).astype(x_blk.dtype)
        carry_in = jnp.einsum("in,hpn->ihp", c_blk, states, precision=HIGH)
        output = within + carry_in * (jnp.exp(log_decay).T * alive_mask[:, None])[:, :, None]
        ending = (seg_blk == seg_blk[-1]).astype(x_blk.dtype)
        tail_weight = jnp.exp(log_decay[:, -1:] - log_decay).T * ending[:, None] * dt_blk
        fresh_state = jnp.einsum(
            "jhp,jn->hpn", x_blk * tail_weight[:, :, None], b_blk, precision=HIGH
        )
        new_states = (
            states * (jnp.exp(log_decay[:, -1]) * alive_mask[-1])[:, None, None] + fresh_state
        )
        return ((new_states, seg_blk[-1]), output)

    start_carry = (
        jnp.zeros((head_count, head_size, nstate), x_heads.dtype),
        jnp.array(-1, jnp.int32),
    )
    final_carry, block_outs = lax.scan(
        jax.checkpoint(advance),
        start_carry,
        (regroup(x_heads), regroup(dt_full), regroup(b_state), regroup(c_state), regroup(segment)),
    )
    return block_outs.reshape(length, head_count, head_size)


def mixer_core(inputs, segment):
    (
        x_raw,
        bc_raw,
        dt_raw,
        gate_raw,
        conv_x,
        conv_x_bias,
        conv_bc,
        conv_bc_bias,
        dt_bias,
        a_log,
        d_skip,
    ) = inputs
    length = x_raw.shape[0]
    full_width = x_raw.shape[1]
    head_count = dt_bias.shape[0]
    head_size = full_width // head_count
    x_act = silu_act(conv_mix(x_raw, conv_x, conv_x_bias, segment))
    bc_act = silu_act(conv_mix(bc_raw, conv_bc, conv_bc_bias, segment))
    nstate = bc_act.shape[1] // 2
    dt_full = jax.nn.softplus(dt_raw + dt_bias[None, :])
    decay_rate = -jnp.exp(a_log)
    x_heads = x_act.reshape(length, head_count, head_size)
    mixed_heads = ssd_scan(
        x_heads, dt_full, decay_rate, bc_act[:, :nstate], bc_act[:, nstate:], segment
    )
    mixed_heads = mixed_heads + d_skip[None, :, None] * x_heads
    return mixed_heads.reshape(length, full_width) * silu_act(gate_raw)


def shards(
    resid,
    cotangent,
    segments,
    pre_gain,
    w_z,
    w_x,
    w_bc,
    w_dt,
    conv_x,
    conv_x_bias,
    conv_bc,
    conv_bc_bias,
    dt_bias,
    a_log,
    d_skip,
    gate_gain,
    w_out,
):
    full_bc, full_gain = (
        lax.all_gather(w_bc, ("dp", "tensor"), axis=0, tiled=True),
        lax.all_gather(pre_gain, ("dp", "tensor"), axis=0, tiled=True),
    )
    full_z, full_x, full_dt, full_out = (
        lax.all_gather(w_z, "dp", axis=0, tiled=True),
        lax.all_gather(w_x, "dp", axis=0, tiled=True),
        lax.all_gather(w_dt, "dp", axis=0, tiled=True),
        lax.all_gather(w_out, "dp", axis=1, tiled=True),
    )
    model_width = resid.shape[1]
    inner_width = gate_gain.shape[0] * lax.axis_size("tensor")
    resid_wide = resid.astype(jnp.float32)
    gain_wide = full_gain.astype(jnp.float32)
    inv_rms = lax.rsqrt(jnp.mean(resid_wide * resid_wide, axis=-1, keepdims=True) + EPS)
    normed_own = (resid_wide * inv_rms * gain_wide[None, :]).astype(jnp.bfloat16)
    normed = lax.all_gather(normed_own, "tensor", axis=0, tiled=True)
    gate_raw = jnp.dot(normed, full_z, preferred_element_type=jnp.float32)
    x_raw = jnp.dot(normed, full_x, preferred_element_type=jnp.float32)
    bc_raw = jnp.dot(normed, full_bc, preferred_element_type=jnp.float32)
    dt_raw = jnp.dot(normed, full_dt, preferred_element_type=jnp.float32)
    core_inputs = (
        x_raw,
        bc_raw,
        dt_raw,
        gate_raw,
        conv_x,
        conv_x_bias,
        conv_bc,
        conv_bc_bias,
        dt_bias,
        a_log,
        d_skip,
    )
    mixed, pullback = jax.vjp(lambda inputs: mixer_core(inputs, segments), core_inputs)
    square_sum = lax.psum(jnp.sum(mixed * mixed, axis=-1), "tensor")
    inv_gate = lax.rsqrt(square_sum / inner_width + EPS)[:, None]
    scaled = (mixed * inv_gate * gate_gain[None, :]).astype(jnp.bfloat16)
    mixer_add = lax.psum_scatter(
        jnp.dot(scaled, full_out, preferred_element_type=jnp.float32).astype(jnp.bfloat16),
        "tensor",
        scatter_dimension=0,
        tiled=True,
    ).astype(jnp.float32)
    layer_out = (resid_wide + mixer_add).astype(jnp.bfloat16)
    cot_full = lax.all_gather(cotangent, "tensor", axis=0, tiled=True)
    grad_w_out = jnp.einsum("ti,td->id", scaled, cot_full, preferred_element_type=jnp.float32)
    grad_scaled = jnp.einsum("td,id->ti", cot_full, full_out, preferred_element_type=jnp.float32)
    grad_gate_gain = jnp.sum(grad_scaled * mixed * inv_gate, axis=0)
    weighted = grad_scaled * gate_gain[None, :]
    dot_total = lax.psum(jnp.sum(weighted * mixed, axis=-1), "tensor")
    grad_mixed = (
        weighted * inv_gate
        - mixed * (inv_gate * inv_gate * inv_gate) * (dot_total / inner_width)[:, None]
    )
    (
        grad_x_raw,
        grad_bc_raw,
        grad_dt_raw,
        grad_gate_raw,
        grad_conv_x,
        grad_conv_x_bias,
        grad_conv_bc,
        grad_conv_bc_bias,
        grad_dt_bias,
        grad_a_log,
        grad_d_skip,
    ) = pullback(grad_mixed)[0]
    gate_low = grad_gate_raw.astype(jnp.bfloat16)
    x_low = grad_x_raw.astype(jnp.bfloat16)
    dt_low = grad_dt_raw.astype(jnp.bfloat16)
    token_term = jnp.einsum("tc,dc->td", gate_low, full_z, preferred_element_type=jnp.float32)
    token_term = token_term + jnp.einsum(
        "tc,dc->td", x_low, full_x, preferred_element_type=jnp.float32
    )
    token_term = token_term + jnp.einsum(
        "tc,dc->td", dt_low, full_dt, preferred_element_type=jnp.float32
    )
    own_term, own_bc = (
        lax.psum_scatter(
            token_term.astype(jnp.bfloat16), "tensor", scatter_dimension=0, tiled=True
        ).astype(jnp.float32),
        lax.psum_scatter(
            grad_bc_raw.astype(jnp.bfloat16), "tensor", scatter_dimension=0, tiled=True
        ).astype(jnp.float32),
    )
    bc_low = own_bc.astype(jnp.bfloat16)
    grad_normed = own_term + jnp.einsum(
        "tc,dc->td", bc_low, full_bc, preferred_element_type=jnp.float32
    )
    grad_w_bc = jnp.einsum("td,tc->dc", normed_own, bc_low, preferred_element_type=jnp.float32)
    grad_w_z = jnp.einsum("td,tc->dc", normed, gate_low, preferred_element_type=jnp.float32)
    grad_w_x = jnp.einsum("td,tc->dc", normed, x_low, preferred_element_type=jnp.float32)
    grad_w_dt = jnp.einsum("td,tc->dc", normed, dt_low, preferred_element_type=jnp.float32)
    grad_w_z, grad_w_x, grad_w_dt, grad_w_out = (
        lax.psum_scatter(grad_w_z, "dp", scatter_dimension=0, tiled=True),
        lax.psum_scatter(grad_w_x, "dp", scatter_dimension=0, tiled=True),
        lax.psum_scatter(grad_w_dt, "dp", scatter_dimension=0, tiled=True),
        lax.psum_scatter(grad_w_out, "dp", scatter_dimension=1, tiled=True),
    )
    grad_pre_gain = jnp.sum(grad_normed * resid_wide * inv_rms, axis=0)
    inner_dot = jnp.sum(gain_wide[None, :] * grad_normed * resid_wide, axis=-1, keepdims=True)
    grad_resid = cotangent.astype(jnp.float32) + gain_wide[None, :] * grad_normed * inv_rms
    grad_resid = grad_resid - resid_wide * (inv_rms * inv_rms * inv_rms) * inner_dot / model_width
    grad_w_bc, grad_pre_gain = (
        lax.psum_scatter(grad_w_bc, ("dp", "tensor"), scatter_dimension=0, tiled=True),
        lax.psum_scatter(grad_pre_gain, ("dp", "tensor"), scatter_dimension=0, tiled=True),
    )
    grad_conv_x, grad_conv_x_bias, grad_dt_bias, grad_a_log, grad_d_skip, grad_gate_gain = lax.psum(
        (grad_conv_x, grad_conv_x_bias, grad_dt_bias, grad_a_log, grad_d_skip, grad_gate_gain), "dp"
    )
    grad_conv_bc, grad_conv_bc_bias = lax.psum((grad_conv_bc, grad_conv_bc_bias), ("dp", "tensor"))
    return (
        layer_out,
        grad_resid,
        grad_pre_gain,
        grad_w_z,
        grad_w_x,
        grad_w_bc,
        grad_w_dt,
        grad_conv_x,
        grad_conv_x_bias,
        grad_conv_bc,
        grad_conv_bc_bias,
        grad_dt_bias,
        grad_a_log,
        grad_d_skip,
        grad_gate_gain,
        grad_w_out,
    )


def solution(mesh):
    return jax.shard_map(
        shards,
        mesh=mesh,
        in_specs=(
            P(("dp", "tensor"), None),
            P(("dp", "tensor"), None),
            P("dp"),
            P(("dp", "tensor")),
            P("dp", "tensor"),
            P("dp", "tensor"),
            P(("dp", "tensor"), None),
            P("dp", "tensor"),
            P(None, "tensor"),
            P("tensor"),
            P(),
            P(),
            P("tensor"),
            P("tensor"),
            P("tensor"),
            P("tensor"),
            P("tensor", "dp"),
        ),
        out_specs=(
            P(("dp", "tensor"), None),
            P(("dp", "tensor"), None),
            P(("dp", "tensor")),
            P("dp", "tensor"),
            P("dp", "tensor"),
            P(("dp", "tensor"), None),
            P("dp", "tensor"),
            P(None, "tensor"),
            P("tensor"),
            P(),
            P(),
            P("tensor"),
            P("tensor"),
            P("tensor"),
            P("tensor"),
            P("tensor", "dp"),
        ),
        check_vma=False,
    )
```

profile of v0, /device:TPU:1, one launch (start us, length us, event | category | flops | bytes accessed | tf_op | source)
XLA Modules:
  0.0 1661.6 jit_solution(6739595070892513604)
XLA Ops:
  10.1 68.8 %all-reduce.23 = bf16[1536]{0:T(1024)(128)(2,1)S(1)} all-reduce(bf16[1536]{0:T(1024)(128)(2,1)S(1)} %dynamic-update-slice), channel_id=1, replica_groups=mesh['dp'=64,'tensor'=2] {'dp','tensor'}, use_global_device_ids=true, to_apply=%add.23 | all-reduce | flops 1536 | bytes 6144
  85.0 93.2 %all_gather.26 = bf16[1536,24]{1,0:T(8,128)(2,1)S(1)} all-gather(bf16[24,24]{1,0:T(8,128)(2,1)S(1)} %copy-done.85), channel_id=1, replica_groups=mesh['dp'=64,'tensor'=2] {'dp'}, dimensions={0}, use_global_device_ids=true | all-gather | bytes 74880 | tf_op jit(solution)/shard_map/all_gather | solution.py:137
  178.1 317.3 %all-gather = bf16[128,12,256]{2,1,0:T(8,128)(2,1)S(1)} all-gather(bf16[1,12,256]{2,1,0:T(8,128)(2,1)S(1)} %bitcast.456), channel_id=1, replica_groups=mesh['dp'=64,'tensor'=2] {'dp','tensor'}, dimensions={0}, use_global_device_ids=true | all-gather | bytes 792576 | tf_op jit(solution)/shard_map/all_gather | solution.py:131
  517.6 6.2 copy.154
  525.9 38.6 %while.45 = (s32[]{:T(128)}, f32[24,64,128]{2,1,0:T(8,128)S(1)}, s32[]{:T(128)}, f32[2,256,24,64]{1,3,2,0:T(8,128)}, f32[2,24,64,128]{3,2,1,0:T(8,128)}, /*index...) while((s32[]{:T(128)}, f32[24,64,128]{2,1,0:T(8,128)S(1)}, ...), condition=%wide.region_4.5_spmd.clone, body=%wide.region_1.4_spmd.clone.sunk | while | flops 2527636480 | bytes 51183192 | solution.py:72
  531.4 8.9 fusion.260
  550.8 8.9 fusion.260
  571.2 6.7 reshape.483
  578.0 9.9 multiply_reduce_fusion.10
  591.7 8.7 multiply_reduce_fusion.3
  604.2 8.3 multiply_reduce_fusion.4
  618.0 6.1 copy.160
  628.2 120.6 %while.46 = (s32[]{:T(128)}, f32[24]{0:T(128)}, f32[24,64,128]{2,1,0:T(8,128)}, f32[2,256,24,64]{1,3,2,0:T(8,128)}, f32[2,256,24]{1,0,2:T(2,128)}, /*index=5*/f3...) while((s32[]{:T(128)}, f32[24]{0:T(128)}, ...), condition=%wide.region_24.25_spmd.clone, body=%wide.region_10.24_spmd.clone.sunk | while | flops 5782014976 | bytes 96906744 | solution.py:72
  644.5 13.0 fusion.280
  705.1 13.0 fusion.280
  759.0 6.4 reshape.485
  765.4 9.3 multiply_reduce_fusion.8
  787.4 7.2 convolution_convert_fusion
  796.5 7.3 fusion.151
  819.6 339.6 %fusion.4 = f32[16,256]{1,0:T(8,128)S(1)} fusion(f32[1536,256]{1,0:T(8,128)S(1)} %fusion.166), kind=kCustom, calls=%all-reduce-scatter | all-reduce-scatter fusion | flops 524289 | bytes 1589248
  1163.3 6.1 collective-permute-start.28
  1176.0 12.9 collective-permute-start.22
  1250.0 324.7 %all-reduce.29 = (f32[4,1536]{1,0:T(4,128)}, f32[1536]{0:T(1024)}, f32[24]{0:T(128)}, f32[24]{0:T(128)}, f32[24]{0:T(128)}, /*index=5*/f32[1536]{0:T(1024)}) all-reduce(f32[4,1536]{1,0:T(4,128)S(1)} %pad_add_fusion.6, f32[1536]{0:T(1024)S(1)} %get-tuple-element.766, ...), channel_id=1, replica_groups=mesh['dp'=64,'tensor'=2] {'dp'}, use_global_device_ids=true, to_apply=%region_38.39 | all-reduce | flops 9288 | bytes 74304 | tf_op jit(solution)/shard_map/psum | solution.py:238
  1581.2 69.6 %all-reduce.28 = (f32[1536]{0:T(1024)S(1)}, f32[4,256]{1,0:T(4,128)}, f32[256]{0:T(256)}) all-reduce(f32[1536]{0:T(1024)S(1)} %get-tuple-element.767, f32[4,256]{1,0:T(4,128)S(1)} %pad_add_fusion.7, f32[256]{0:T(256)S(1)} %get-tuple-element.773), channel_id=5, replica_groups=mesh['dp'=64,'tensor'=2] {'dp','tensor'}, use_global_device_ids=true, to_apply=%region_29.30.clone | all-reduce | flops 2816 | bytes 22528
  (547 shorter events, 291.0 us)
Async XLA Ops:
  7.3 489.2 %all-gather.7.cloned.1.call-start = ((), (), s32[]{:S(2)}) async-start(), calls=%async_computation.7 | async-start | bytes 2359296 | tf_op jit(solution)/shard_map/all_gather | solution.py:146
  81.7 421.0 %all-gather.9.cloned.1.call-start = ((), (), s32[]{:S(2)}) async-start(), calls=%async_computation.8 | async-start | bytes 4792320 | tf_op jit(solution)/shard_map/all_gather | solution.py:136
  82.5 495.5 %all-gather.11.cloned.1.call-start = ((), (), s32[]{:S(2)}) async-start(), calls=%async_computation.9 | async-start | bytes 4792320 | tf_op jit(solution)/shard_map/all_gather | solution.py:135
  83.2 508.4 %all-gather.15.cloned.1.call-start = ((), (), s32[]{:S(2)}) async-start(), calls=%async_computation.12 | async-start | bytes 2359296 | tf_op jit(solution)/shard_map/all_gather | solution.py:175
  83.8 507.9 %all-gather.13.cloned.1.call-start = ((), (), s32[]{:S(2)}) async-start(), calls=%async_computation.10 | async-start | bytes 4792320 | tf_op jit(solution)/shard_map/all_gather | solution.py:138
  84.4 732.8 %reduce-scatter.16.cloned.1.call-start = ((), (), s32[]{:S(2)}) async-start(), calls=%async_computation.14 | async-start | bytes 393216 | tf_op jit(solution)/shard_map/reduce_scatter | solution.py:212
  754.6 824.4 %reduce-scatter.14.cloned.1.call-start = ((), (), s32[]{:S(2)}) async-start(), calls=%async_computation.13 | async-start | bytes 2359296 | tf_op jit(solution)/shard_map/reduce_scatter | solution.py:209
  787.3 864.1 %reduce-scatter.12.cloned.1.call-start = ((), (), s32[]{:S(2)}) async-start(), calls=%async_computation.11 | async-start | bytes 2359296 | tf_op jit(solution)/shard_map/reduce_scatter | solution.py:168
  794.6 859.9 %reduce-scatter.24.cloned.1.call-start = ((), (), s32[]{:S(2)}) async-start(), calls=%async_computation.18 | async-start | bytes 798720
  796.4 858.2 %reduce-scatter.22.cloned.1.call-start = ((), (), s32[]{:S(2)}) async-start(), calls=%async_computation.17 | async-start | bytes 9584640 | tf_op jit(solution)/shard_map/reduce_scatter | solution.py:228
  803.8 850.8 %reduce-scatter.18.cloned.1.call-start = ((), (), s32[]{:S(2)}) async-start(), calls=%async_computation.15 | async-start | bytes 9584640 | tf_op jit(solution)/shard_map/reduce_scatter | solution.py:225
  810.5 844.1 %reduce-scatter.20.cloned.1.call-start = ((), (), s32[]{:S(2)}) async-start(), calls=%async_computation.16 | async-start | bytes 9584640 | tf_op jit(solution)/shard_map/reduce_scatter | solution.py:226
  1170.7 18.1 %collective-permute-start.26 = (f32[16,256]{1,0:T(8,128)S(1)}, f32[16,256]{1,0:T(8,128)S(1)}, u32[]{:S(2)}, u32[]{:S(2)}) collective-permute-start(f32[16,256]{1,0:T(8,128)S(1)} %fusion.4), channel_id=1, source_target_pairs={{0,27},{1,28},{2,29},{3,30},{4,31},{5,32},{6,33},{7,34},{8,35},{9,... | collective-permute-start | bytes 49160
  1172.0 21.0 %collective-permute-start.25 = (f32[16,256]{1,0:T(8,128)S(1)}, f32[16,256]{1,0:T(8,128)S(1)}, u32[]{:S(2)}, u32[]{:S(2)}) collective-permute-start(f32[16,256]{1,0:T(8,128)S(1)} %fusion.4), channel_id=1, source_target_pairs={{0,26},{1,27},{2,28},{3,29},{4,30},{5,31},{6,32},{7,33},{8,34},{9,... | collective-permute-start | bytes 49160
  1173.3 21.9 %collective-permute-start.24 = (f32[16,256]{1,0:T(8,128)S(1)}, f32[16,256]{1,0:T(8,128)S(1)}, u32[]{:S(2)}, u32[]{:S(2)}) collective-permute-start(f32[16,256]{1,0:T(8,128)S(1)} %fusion.4), channel_id=1, source_target_pairs={{0,25},{1,26},{2,27},{3,28},{4,29},{5,30},{6,31},{7,32},{8,33},{9,... | collective-permute-start | bytes 49160
  1174.6 22.9 %collective-permute-start.23 = (f32[16,256]{1,0:T(8,128)S(1)}, f32[16,256]{1,0:T(8,128)S(1)}, u32[]{:S(2)}, u32[]{:S(2)}) collective-permute-start(f32[16,256]{1,0:T(8,128)S(1)} %fusion.4), channel_id=1, source_target_pairs={{0,24},{1,25},{2,26},{3,27},{4,28},{5,29},{6,30},{7,31},{8,32},{9,... | collective-permute-start | bytes 49160
  1176.0 22.9 %collective-permute-start.22 = (f32[16,256]{1,0:T(8,128)S(1)}, f32[16,256]{1,0:T(8,128)S(1)}, u32[]{:S(2)}, u32[]{:S(2)}) collective-permute-start(f32[16,256]{1,0:T(8,128)S(1)} %fusion.4), channel_id=1, source_target_pairs={{0,23},{1,24},{2,25},{3,26},{4,27},{5,28},{6,29},{7,30},{8,31},{9,... | collective-permute-start | bytes 49160
  1215.0 16.9 %collective-permute-start.10 = (f32[16,256]{1,0:T(8,128)S(1)}, f32[16,256]{1,0:T(8,128)S(1)}, u32[]{:S(2)}, u32[]{:S(2)}) collective-permute-start(f32[16,256]{1,0:T(8,128)S(1)} %fusion.4), channel_id=1, source_target_pairs={{0,11},{1,12},{2,13},{3,14},{4,15},{5,16},{6,17},{7,18},{8,19},{9,... | collective-permute-start | bytes 49160
  1227.3 16.7 %collective-permute-start.6 = (f32[16,256]{1,0:T(8,128)S(1)}, f32[16,256]{1,0:T(8,128)S(1)}, u32[]{:S(2)}, u32[]{:S(2)}) collective-permute-start(f32[16,256]{1,0:T(8,128)S(1)} %fusion.4), channel_id=1, source_target_pairs={{0,7},{1,8},{2,9},{3,10},{4,11},{5,12},{6,13},{7,14},{8,15},{9,16}... | collective-permute-start | bytes 49160
  1234.7 340.0 %collective-permute-start.4 = (f32[16,256]{1,0:T(8,128)S(1)}, f32[16,256]{1,0:T(8,128)S(1)}, u32[]{:S(2)}, u32[]{:S(2)}) collective-permute-start(f32[16,256]{1,0:T(8,128)S(1)} %fusion.4), channel_id=1, source_target_pairs={{0,5},{1,6},{2,7},{3,8},{4,9},{5,10},{6,11},{7,12},{8,13},{9,14},{... | collective-permute-start | bytes 49160
  1236.0 338.7 %collective-permute-start.3 = (f32[16,256]{1,0:T(8,128)S(1)}, f32[16,256]{1,0:T(8,128)S(1)}, u32[]{:S(2)}, u32[]{:S(2)}) collective-permute-start(f32[16,256]{1,0:T(8,128)S(1)} %fusion.4), channel_id=1, source_target_pairs={{0,4},{1,5},{2,6},{3,7},{4,8},{5,9},{6,10},{7,11},{8,12},{9,13},{1... | collective-permute-start | bytes 49160
  1240.1 334.6 %collective-permute-start.2 = (f32[16,256]{1,0:T(8,128)S(1)}, f32[16,256]{1,0:T(8,128)S(1)}, u32[]{:S(2)}, u32[]{:S(2)}) collective-permute-start(f32[16,256]{1,0:T(8,128)S(1)} %fusion.4), channel_id=1, source_target_pairs={{0,3},{1,4},{2,5},{3,6},{4,7},{5,8},{6,9},{7,10},{8,11},{9,12},{10... | collective-permute-start | bytes 49160
  1244.0 330.7 %collective-permute-start.1 = (f32[16,256]{1,0:T(8,128)S(1)}, f32[16,256]{1,0:T(8,128)S(1)}, u32[]{:S(2)}, u32[]{:S(2)}) collective-permute-start(f32[16,256]{1,0:T(8,128)S(1)} %fusion.4), channel_id=1, source_target_pairs={{0,2},{1,3},{2,4},{3,5},{4,6},{5,7},{6,8},{7,9},{8,10},{9,11},{10,... | collective-permute-start | bytes 49160
  1246.8 327.9 %collective-permute-start = (f32[16,256]{1,0:T(8,128)S(1)}, f32[16,256]{1,0:T(8,128)S(1)}, u32[]{:S(2)}, u32[]{:S(2)}) collective-permute-start(f32[16,256]{1,0:T(8,128)S(1)} %fusion.4), channel_id=1, source_target_pairs={{0,1},{1,2},{2,3},{3,4},{4,5},{5,6},{6,7},{7,8},{8,9},{9,10},{10,1... | collective-permute-start | bytes 49160
  (145 other events, 13195.8 us)
Sparse Core Ops, SparseCore 0:
  81.8 26.5 all-gather.6
  111.6 74.3 all-gather.8
  189.2 72.4 all-gather.10
  263.2 29.2 all-gather.14
  295.5 74.7 all-gather.12
  754.7 14.3 reduce-scatter.15
  787.4 28.8 reduce-scatter.13
  818.6 30.9 reduce-scatter.11
  856.1 142.5 reduce-scatter.23
  1004.9 171.1 reduce-scatter.21
  1183.4 168.3 reduce-scatter.17
  1358.0 168.5 reduce-scatter.19
where the time goes:
time: 1670 us; the launch traced here: 1660 us
  blocking collectives  1220 us (73%)
  matrix products  166 us (10%)
  local copies, waits for them, and re-layouts  95.5 us (6%)
  starting transfers between devices  90.6 us (5%)
  other arithmetic  67.6 us (4%)
    unnamed x3, blocking collectives  478 us
    psum x1, blocking collectives, shards(): lax.psum((grad_conv_x, grad_conv_x_bias, grad_dt_bias, grad_a_log, grad_d...  325 us
    all_gather x1, blocking collectives, shards(): lax.all_gather(w_bc, ('dp', 'tensor'), axis=0, tiled=True)  317 us
    all_gather x1, blocking collectives, shards(): lax.all_gather(w_dt, 'dp', axis=0, tiled=True)  93.2 us
    unnamed x33, starting transfers between devices  90.1 us
    dot_general x6, matrix products, advance(): within = jnp.einsum('hij,jhp->ihp', mixing, x_blk, precision=HIGH)  54.9 us
  transfers between devices with their start and end apart: 44, of which 0 were waited for; matrix products, arithmetic and copies ran while one was open for 30% of the time, Pallas kernels for 0%

commit v1 on v0

v1 whole, which is shorter than its diff:
```python
import jax
import jax.numpy as jnp
from jax import lax
from jax.sharding import Mesh, PartitionSpec as P

GROUP = 256
EPS = 1e-05
HIGH = lax.Precision.HIGHEST
BF = jnp.bfloat16
F32 = jnp.float32


def silu_act(values):
    return values * jax.nn.sigmoid(values)


def conv_mix(values, kernel, conv_bias, segment):
    kernel_size = kernel.shape[0]
    row_count = values.shape[0]
    padded = jnp.concatenate(
        [jnp.zeros((kernel_size - 1, values.shape[1]), values.dtype), values], axis=0
    )
    seg_pad = jnp.concatenate([jnp.full((kernel_size - 1,), -1, jnp.int32), segment], axis=0)
    summed = jnp.broadcast_to(conv_bias[None, :], values.shape)
    for offset in range(kernel_size):
        window = padded[offset : offset + row_count]
        keep_mask = (seg_pad[offset : offset + row_count] == segment).astype(values.dtype)
        summed = summed + window * kernel[offset][None, :] * keep_mask[:, None]
    return summed


def ssd_scan(x_heads, dt_full, decay_rate, b_state, c_state, segment):
    length = x_heads.shape[0]
    head_count = x_heads.shape[1]
    head_size = x_heads.shape[2]
    nstate = b_state.shape[1]
    blocks = length // GROUP
    row_ids = lax.broadcasted_iota(jnp.int32, (GROUP, GROUP), 0)
    col_ids = lax.broadcasted_iota(jnp.int32, (GROUP, GROUP), 1)
    causal = row_ids >= col_ids

    def regroup(values):
        return values.reshape((blocks, GROUP) + values.shape[1:])

    def advance(carried, pieces):
        states, last_seg = carried
        x_blk, dt_blk, b_blk, c_blk, seg_blk = pieces
        log_decay = jnp.cumsum(dt_blk * decay_rate[None, :], axis=0).T
        log_gaps = log_decay[:, :, None] - log_decay[:, None, :]
        inside = causal & (seg_blk[:, None] == seg_blk[None, :])
        decays = jnp.where(inside[None], jnp.exp(jnp.minimum(log_gaps, 0.0)), 0.0)
        scores = jnp.einsum("in,jn->ij", c_blk, b_blk, precision=HIGH)
        mixing = decays * scores[None] * dt_blk.T[:, None, :]
        within = jnp.einsum("hij,jhp->ihp", mixing, x_blk, precision=HIGH)
        alive_mask = (seg_blk == last_seg).astype(x_blk.dtype)
        carry_in = jnp.einsum("in,hpn->ihp", c_blk, states, precision=HIGH)
        output = within + carry_in * (jnp.exp(log_decay).T * alive_mask[:, None])[:, :, None]
        ending = (seg_blk == seg_blk[-1]).astype(x_blk.dtype)
        tail_weight = jnp.exp(log_decay[:, -1:] - log_decay).T * ending[:, None] * dt_blk
        fresh_state = jnp.einsum(
            "jhp,jn->hpn", x_blk * tail_weight[:, :, None], b_blk, precision=HIGH
        )
        new_states = (
            states * (jnp.exp(log_decay[:, -1]) * alive_mask[-1])[:, None, None] + fresh_state
        )
        return ((new_states, seg_blk[-1]), output)

    start_carry = (
        jnp.zeros((head_count, head_size, nstate), x_heads.dtype),
        jnp.array(-1, jnp.int32),
    )
    final_carry, block_outs = lax.scan(
        jax.checkpoint(advance),
        start_carry,
        (regroup(x_heads), regroup(dt_full), regroup(b_state), regroup(c_state), regroup(segment)),
    )
    return block_outs.reshape(length, head_count, head_size)


def mixer_core(inputs, segment):
    (x_raw, bc_raw, dt_raw, gate_raw, conv_x, conv_x_bias, conv_bc, conv_bc_bias, dt_bias, a_log, d_skip) = inputs
    length, full_width = x_raw.shape
    head_count = dt_bias.shape[0]
    x_act = silu_act(conv_mix(x_raw, conv_x, conv_x_bias, segment))
    bc_act = silu_act(conv_mix(bc_raw, conv_bc, conv_bc_bias, segment))
    nstate = bc_act.shape[1] // 2
    dt_full = jax.nn.softplus(dt_raw + dt_bias[None, :])
    decay_rate = -jnp.exp(a_log)
    x_heads = x_act.reshape(length, head_count, full_width // head_count)
    mixed_heads = ssd_scan(x_heads, dt_full, decay_rate, bc_act[:, :nstate], bc_act[:, nstate:], segment)
    mixed_heads = mixed_heads + d_skip[None, :, None] * x_heads
    return mixed_heads.reshape(length, full_width) * silu_act(gate_raw)


def swap(a, axis):
    return lax.ppermute(a, axis, [(0, 1), (1, 0)])


def turn(a, axis, k):
    return lax.ppermute(a, axis, [(i, (i + k) % 4) for i in range(4)])


def pair(own, other, axis):
    first = lax.axis_index(axis) == 0
    return jnp.stack([jnp.where(first, own, other), jnp.where(first, other, own)])


def mine(a, axis, dim, size):
    i = lax.axis_index(axis)
    return (
        lax.dynamic_slice_in_dim(a, i * size, size, dim),
        lax.dynamic_slice_in_dim(a, (1 - i) * size, size, dim),
    )


def gather4(blk, axis, dim):
    i = lax.axis_index(axis)
    got = [blk, turn(blk, axis, 1), turn(blk, axis, 2), turn(blk, axis, 3)]
    shape = blk.shape[:dim] + (4,) + blk.shape[dim:]
    out = jnp.zeros(shape, blk.dtype)
    for k, piece in enumerate(got):
        out = lax.dynamic_update_slice_in_dim(out, jnp.expand_dims(piece, dim), (i - k) % 4, dim)
    return out


def gather_chips(blk, order):
    b = pair(blk, swap(blk, "xh"), "xh")
    if order == "yz":
        b = gather4(gather4(b, "y", 1), "z", 0)
    else:
        b = gather4(gather4(b, "z", 0), "y", 2)
    return b.reshape(1536, blk.shape[1])


def reduce4(a, axis, dim):
    i = lax.axis_index(axis)

    def entry(k):
        return lax.squeeze(lax.dynamic_slice_in_dim(a, (i + k) % 4, 1, dim), (dim,))

    total = entry(0).astype(F32)
    for k in (1, 2, 3):
        total = total + turn(entry(k), axis, k).astype(F32)
    return total


def reduce_chips(g, order):
    b = g.reshape(4, 2, 4, 48, g.shape[1])
    if order == "yz":
        b = reduce4(b, "y", 2).astype(BF)
        b = reduce4(b, "z", 0).astype(BF)
    else:
        b = reduce4(b, "z", 0).astype(BF)
        b = reduce4(b, "y", 1).astype(BF)
    own, other = mine(b, "xh", 0, 1)
    return own[0].astype(F32) + swap(other[0], "xh").astype(F32)


def sum_chips(a):
    a = a + swap(a, "xh")
    a = a + turn(a, "y", 1) + turn(a, "y", 2) + turn(a, "y", 3)
    return a + turn(a, "z", 1) + turn(a, "z", 2) + turn(a, "z", 3)


def shards(resid, cotangent, segments, pre_gain, w_z, w_x, w_bc, w_dt, conv_x, conv_x_bias, conv_bc, conv_bc_bias, dt_bias, a_log, d_skip, gate_gain, w_out):
    core = lax.axis_index("c")
    def group_tokens(a):
        half = pair(a, swap(a, "xl"), "xl").reshape(512, a.shape[1])
        return pair(half, swap(half, "c"), "c")

    def quarter(a, size):
        own, other = mine(a, "c", 1, size)
        return pair(own, swap(other, "c"), "c").reshape(48, size)

    bc_rows = pair(w_bc, swap(w_bc, "xl"), "xl").reshape(24, 256)
    gain_rows = pair(pre_gain[:, None], swap(pre_gain[:, None], "xl"), "xl").reshape(24, 1)
    bc_rows = pair(bc_rows, swap(bc_rows, "c"), "c").reshape(48, 256)
    gain_rows = pair(gain_rows, swap(gain_rows, "c"), "c").reshape(48, 1)
    wx_q, wz_q, wo_q, wdt_q = quarter(w_x, 768), quarter(w_z, 768), quarter(w_out.T, 768), quarter(w_dt, 12)
    side = jnp.concatenate([wdt_q, gain_rows, jnp.zeros((48, 115), BF)], axis=1)
    first = jnp.concatenate([wx_q, bc_rows, side], axis=1)
    full_a = gather_chips(first[:, :512], "yz")
    full_b = gather_chips(first[:, 512:], "zy")
    full_z = gather_chips(wz_q, "yz")
    full_o = gather_chips(wo_q, "zy")
    full_1 = jnp.concatenate([full_a, full_b], axis=1)
    full_x, full_bc, full_dt, full_gain = full_1[:, :768], full_1[:, 768:1024], full_1[:, 1024:1036], full_1[:, 1036]

    tokens = group_tokens(resid).reshape(1024, 1536)
    cot = group_tokens(cotangent).reshape(1024, 1536)
    seg = pair(segments, swap(segments, "c"), "c")

    gain_wide = full_gain.astype(F32)
    wide = tokens.astype(F32)
    inv_all = lax.rsqrt(jnp.mean(wide * wide, axis=-1, keepdims=True) + EPS)
    normed = (wide * inv_all * gain_wide[None, :]).astype(BF)

    def dot(a, b):
        return jnp.dot(a, b, preferred_element_type=F32)

    gate_raw, x_raw, bc_raw, dt_raw = dot(normed, full_z), dot(normed, full_x), dot(normed, full_bc), dot(normed, full_dt)

    def own(a, size):
        return mine(a, "c", a.ndim - 1, size)[0]

    cx, cxb, gg = own(conv_x, 768), own(conv_x_bias, 768), own(gate_gain, 768)
    dtb, al, dsk = own(dt_bias, 12), own(a_log, 12), own(d_skip, 12)

    def core_fn(inputs):
        x, bc, dt, gate, *params = inputs
        r = lambda a: a.reshape(2, 512, a.shape[-1])
        f = lambda x, bc, dt, gate, s: mixer_core((x, bc, dt, gate, *params), s)
        return jax.vmap(f)(r(x), r(bc), r(dt), r(gate), seg).reshape(1024, 768)

    mixed, pullback = jax.vjp(core_fn, (x_raw, bc_raw, dt_raw, gate_raw, cx, cxb, conv_bc, conv_bc_bias, dtb, al, dsk))
    grad_scaled = lax.dot_general(cot, full_o, (((1,), (0,)), ((), ())), preferred_element_type=F32)
    weighted = grad_scaled * gg[None, :]
    sums = jnp.stack([jnp.sum(mixed * mixed, axis=-1), jnp.sum(weighted * mixed, axis=-1)])
    sums = sums + swap(sums, "c")
    sums = sums + swap(sums, "xl")
    inv_gate = lax.rsqrt(sums[0] / 3072 + EPS)[:, None]
    scaled = (mixed * inv_gate * gg[None, :]).astype(BF)
    out_part = lax.dot_general(scaled, full_o, (((1,), (1,)), ((), ())), preferred_element_type=F32).astype(BF)

    def scatter_tokens(a):
        a = a.reshape(2, 512, a.shape[1])
        keep, send = mine(a, "c", 0, 1)
        half = (keep[0].astype(F32) + swap(send[0], "c").astype(F32)).astype(BF)
        keep, send = mine(half, "xl", 0, 256)
        return keep.astype(F32) + swap(send, "xl").astype(F32)

    layer_out = (resid.astype(F32) + scatter_tokens(out_part)).astype(BF)

    def over_tokens(a, b):
        return lax.dot_general(a, b, (((0,), (0,)), ((), ())), preferred_element_type=F32)

    g_out = reduce_chips(over_tokens(cot, scaled).astype(BF), "yz")
    g_gain = jnp.sum(grad_scaled * mixed * inv_gate, axis=0)
    grad_mixed = weighted * inv_gate - mixed * (inv_gate * inv_gate * inv_gate) * (sums[1] / 3072)[:, None]
    (gx, gbc, gdt, gz, g_cx, g_cxb, g_cbc, g_cbcb, g_dtb, g_al, g_dsk) = pullback(grad_mixed)[0]
    gate_low, x_low, dt_low = gz.astype(BF), gx.astype(BF), gdt.astype(BF)
    g_z = reduce_chips(over_tokens(normed, gate_low).astype(BF), "zy")

    keep, send = mine(gbc.astype(BF), "c", 1, 128)
    half = (keep.astype(F32) + swap(send, "c").astype(F32)).astype(BF)
    keep, send = mine(half, "xl", 1, 64)
    bc_low = (keep.astype(F32) + swap(send, "xl").astype(F32)).astype(BF)
    q = core * 2 + lax.axis_index("xl")
    bc_q = lax.dynamic_slice_in_dim(full_bc, q * 64, 64, 1)
    side_w = jnp.concatenate([full_x, bc_q, full_dt, jnp.zeros((1536, 52), BF)], axis=1)
    side_g = jnp.concatenate([x_low, bc_low, dt_low, jnp.zeros((1024, 52), BF)], axis=1)
    nt = lambda a, b: lax.dot_general(a, b, (((1,), (1,)), ((), ())), preferred_element_type=F32)
    token_term = nt(gate_low, full_z) + nt(side_g, side_w)
    grad_normed = scatter_tokens(token_term.astype(BF))
    g_side_full = over_tokens(normed, side_g).astype(BF)
    g_side = jnp.concatenate([reduce_chips(g_side_full[:, :512], "yz"), reduce_chips(g_side_full[:, 512:], "zy")], axis=1)

    rw = resid.astype(F32)
    inv = lax.rsqrt(jnp.mean(rw * rw, axis=-1, keepdims=True) + EPS)
    inner = jnp.sum(gain_wide[None, :] * grad_normed * rw, axis=-1, keepdims=True)
    grad_resid = cotangent.astype(F32) + gain_wide[None, :] * grad_normed * inv - rw * (inv * inv * inv) * inner / 1536

    def spread(a):
        keep, send = mine(a, "c", 0, 24)
        got = pair(keep, swap(send, "c"), "c")
        return jnp.concatenate([got[0], got[1]], axis=1)

    grad_w_z, grad_w_x, grad_w_dt = spread(g_z), spread(g_side[:, :768]), spread(g_side[:, 832:844])
    grad_w_out_t = spread(g_out)
    bc24 = spread(g_side[:, 768:832]).reshape(24, 2, 64)
    keep, send = mine(bc24, "xl", 0, 12)
    got = pair(keep, swap(send, "xl"), "xl")
    grad_w_bc = got.transpose(1, 2, 0, 3).reshape(12, 256)

    tall = lambda a, b: jnp.sum(a.astype(F32) * b, axis=1)
    pg = tall(w_z, grad_w_z) + tall(w_x, grad_w_x) + tall(w_dt, grad_w_dt)
    pg_keep, pg_send = mine(pg, "xl", 0, 12)
    pg = pg_keep + swap(pg_send, "xl") + tall(w_bc, grad_w_bc)
    grad_pre_gain = pg / pre_gain.astype(F32)

    small = jnp.concatenate([g_cx.reshape(-1), g_cxb, g_gain, g_dtb, g_al, g_dsk, g_cbc.reshape(-1), g_cbcb])
    small = sum_chips(small)
    nx = 6 * 768 + 36
    cbc = small[nx:]
    cbc = cbc + swap(cbc, "c")
    cbc = cbc + swap(cbc, "xl")
    both = pair(small[:nx], swap(small[:nx], "c"), "c")
    grad_conv_x = both[:, :3072].reshape(2, 4, 768).transpose(1, 0, 2).reshape(4, 1536)
    pick = lambda a, n: both[:, a : a + n].reshape(-1)
    return (
        layer_out,
        grad_resid,
        grad_pre_gain,
        grad_w_z,
        grad_w_x,
        grad_w_bc,
        grad_w_dt,
        grad_conv_x,
        pick(3072, 768),
        cbc[:1024].reshape(4, 256),
        cbc[1024:],
        pick(4608, 12),
        pick(4620, 12),
        pick(4632, 12),
        pick(3840, 768),
        grad_w_out_t.T,
    )


def solution(mesh):
    fine = Mesh(mesh.devices.reshape(4, 2, 4, 2, 2), ("z", "xh", "y", "c", "xl"))
    dp, tp, every = ("z", "xh", "y", "c"), "xl", ("z", "xh", "y", "c", "xl")
    return jax.shard_map(
        shards,
        mesh=fine,
        in_specs=(P(every, None), P(every, None), P(dp), P(every), P(dp, tp), P(dp, tp), P(every, None), P(dp, tp), P(None, tp), P(tp), P(), P(), P(tp), P(tp), P(tp), P(tp), P(tp, dp)),
        out_specs=(P(every, None), P(every, None), P(every), P(dp, tp), P(dp, tp), P(every, None), P(dp, tp), P(None, tp), P(tp), P(), P(), P(tp), P(tp), P(tp), P(tp), P(tp, dp)),
        check_vma=False,
    )
```

time: 1670 us -> 798 us (0.48)
  blocking collectives: 1220 us -> 0 us
  waiting for transfers between devices: 2.77 us -> 113 us
  local copies, waits for them, and re-layouts: 95.5 us -> 203 us
  other arithmetic: 67.6 us -> 154 us
  starting transfers between devices: 90.6 us -> 138 us
    unnamed x3 -> x0, blocking collectives: 478 us -> none
    all_gather x2 -> x0, blocking collectives: 410 us -> none  [the longest x1 317 us: shards(): lax.all_gather(w_bc, ('dp', 'tensor'), axis=0, tiled=True)]
    psum x3 -> x0, blocking collectives: 332 us -> none  [the longest x1 325 us: shards(): lax.psum((grad_conv_x, grad_conv_x_bias, grad_dt_bias, grad_a_log, grad_d...]
    ppermute x0 -> x94, starting transfers between devices: none -> 138 us  [the longest x54 74.2 us: turn(): return lax.ppermute(a, axis, [(i, (i + k) % 4) for i in range(4)])]
    ppermute x0 -> x94, waiting for transfers between devices: none -> 113 us  [the longest x54 62.5 us: turn(): return lax.ppermute(a, axis, [(i, (i + k) % 4) for i in range(4)])]
    unnamed x33 -> x0, starting transfers between devices: 90.1 us -> none
    another operation x23 -> x60, other arithmetic: 10.6 us -> 45.9 us
    another operation x18 -> x50, local copies, waits for them, and re-layouts: 6.43 us -> 37.2 us
  transfers between devices with their start and end apart: 44 -> 94, of which waited for: 0 -> 35; matrix products, arithmetic and copies ran while one was open for 30% -> 50% of each run, Pallas kernels for 0% -> 0%
where the time goes in v1:
time: 798 us; the launch traced here: 783 us
  local copies, waits for them, and re-layouts  203 us (25%)
  matrix products  163 us (20%)
  other arithmetic  154 us (19%)
  starting transfers between devices  138 us (17%)
  waiting for transfers between devices  113 us (14%)
  loops' own time  9.72 us (1%)
    ppermute x54, starting transfers between devices, turn(): return lax.ppermute(a, axis, [(i, (i + k) % 4) for i in range(4)])  74.2 us
    ppermute x40, starting transfers between devices, swap(): return lax.ppermute(a, axis, [(0, 1), (1, 0)])  63.5 us
    ppermute x54, waiting for transfers between devices, turn(): return lax.ppermute(a, axis, [(i, (i + k) % 4) for i in range(4)])  62.5 us
    dot_general x6, matrix products, advance(): within = jnp.einsum('hij,jhp->ihp', mixing, x_blk, precision=HIGH)  56.8 us
    ppermute x40, waiting for transfers between devices, swap(): return lax.ppermute(a, axis, [(0, 1), (1, 0)])  50.4 us
    another operation x43, local copies, waits for them, and re-layouts  30.2 us
    another operation x23, other arithmetic  28.7 us
    dot_general x8, matrix products, advance(): carry_in = jnp.einsum('in,hpn->ihp', c_blk, states, precision=HIGH)  24.8 us
  transfers between devices with their start and end apart: 94, of which 35 were waited for; matrix products, arithmetic and copies ran while one was open for 50% of the time, Pallas kernels for 0%

profile of v1, /device:TPU:1, one launch (start us, length us, event | category | flops | bytes accessed | tf_op | source)
XLA Modules:
  0.0 783.3 jit_solution(7144888394411702121)
XLA Ops:
  36.4 9.5 %collective-permute-done.16 = bf16[48,512]{1,0:T(8,128)(2,1)S(1)} collective-permute-done((bf16[48,512]{1,0:T(8,128)(2,1)S(1)}, bf16[48,512]{1,0:T(8,128)(2,1)S(1)}, u32[]{:S(2)}, u32[]{:S(2)}) %collective-permute-start.16) | collective-permute-done | bytes 49184 | tf_op jit(solution)/shard_map/ppermute | solution.py:96
  79.7 5.2 collective-permute-done.20
  84.9 6.7 collective-permute-done.21
  100.9 6.0 collective-permute-start.29
  107.0 6.7 collective-permute-done.14
  139.6 6.9 collective-permute-done.38
  146.6 12.7 %collective-permute-done.39 = bf16[4,2,48,768]{3,2,1,0:T(8,128)(2,1)S(1)} collective-permute-done((bf16[4,2,48,768]{3,2,1,0:T(8,128)(2,1)S(1)}, bf16[4,2,48,768]{3,2,1,0:T(8,128)(2,1)S(1)}, u32[]{:S(2)}, u32[]{:S(2)}) %collective-permute-start.39) | collective-permute-done | bytes 589856 | tf_op jit(solution)/shard_map/ppermute | solution.py:100
  185.6 5.2 reshape.865
  198.1 44.3 %while.45 = (s32[]{:T(128)}, f32[2,12,64,128]{3,2,1,0:T(8,128)S(1)}, s32[2]{0:T(128)S(1)}, f32[2,2,256,12,64]{2,4,3,1,0:T(8,128)}, f32[2,2,12,64,128]{4,3,2,1,0:...) while((s32[]{:T(128)}, ...), condition=%wide.region_4.5_spmd.clone, body=%wide.region_1.4_spmd.clone.sunk | while | flops 2628419584 | bytes 15223445 | solution.py:72
  201.8 8.6 %fusion.291 = f32[2,12,64,256]{3,2,1,0:T(8,128)S(1)} fusion(f32[2,12,256]{2,1,0:T(8,128)S(1)} %copy.869, f32[2,256,256]{2,1,0:T(8,128)S(1)} %fusion.289, f32[2,12,256]{2,1,0:T(8,128)S(1)} %copy.870, pred[2,256,256]{2,1,0:T(8,128)(4,1)S(1)} %compare_and_fusion.4, f32[2,2,256,12,64]{2,4,3,1,0:T(8,128)} %get-tuple-element.1291, s32[]{:T(128)} %get-tuple-element.1267), kind=kOutput, calls=%fused_computation.2.clone.1 | convolution fusion | flops 1215823872 | bytes 3899904 | tf_op jit(solution)/shard_map/jvp(vmap())/while/body/eval_jaxpr/hij,jhp->ihp/dot_general | solution.py:54
  223.9 8.6 %fusion.291 = f32[2,12,64,256]{3,2,1,0:T(8,128)S(1)} fusion(f32[2,12,256]{2,1,0:T(8,128)S(1)} %copy.869, f32[2,256,256]{2,1,0:T(8,128)S(1)} %fusion.289, f32[2,12,256]{2,1,0:T(8,128)S(1)} %copy.870, pred[2,256,256]{2,1,0:T(8,128)(4,1)S(1)} %compare_and_fusion.4, f32[2,2,256,12,64]{2,4,3,1,0:T(8,128)} %get-tuple-element.1291, s32[]{:T(128)} %get-tuple-element.1267), kind=kOutput, calls=%fused_computation.2.clone.1 | convolution fusion | flops 1215823872 | bytes 3899904 | tf_op jit(solution)/shard_map/jvp(vmap())/while/body/eval_jaxpr/hij,jhp->ihp/dot_general | solution.py:54
  261.3 9.7 %multiply_reduce_fusion.9 = (f32[2,512]{1,0:T(2,128)S(1)}, f32[2,512,768]{2,1,0:T(8,128)S(1)}, f32[2,512,768]{2,1,0:T(8,128)}) fusion(f32[2,512,768]{2,1,0:T(8,128)} %copy.714, f32[2,512,768]{2,1,0:T(8,128)S(1)} %copy-done.6, f32[768]{0:T(1024)S(1)} %copy-done.98, bf16[1536,768,1]{1,0,2:T(8,128)(2,1)} %bitcast.776, f32[1536]{0:T(1024)S(1)} %convert_reduce_fusion, ...), kind=kOutput, calls=%fused_computation.199 | convolution fusion | flops 2434006016 | bytes 18105344 | tf_op jit(solution)/shard_map/dot_general | solution.py:199
  277.1 6.6 copy.743
  321.3 225.3 %while.46 = (s32[]{:T(128)}, f32[12]{0:T(128)}, f32[2,12,64,128]{3,2,1,0:T(8,128)}, f32[2,2,256,12,64]{2,4,3,1,0:T(8,128)}, f32[2,2,256,12]{3,1,2,0:T(2,128)}, /...) while((s32[]{:T(128)}, f32[12]{0:T(128)}, ...), condition=%wide.region_21.22_spmd.clone, body=%wide.region_7.21_spmd.clone.sunk | while | flops 6084093952 | bytes 79042816 | solution.py:72
  368.1 13.0 %fusion.312 = (f32[2,12,256]{2,1,0:T(8,128)}, f32[2,12,256]{2,1,0:T(8,128)}, f32[2,12,256]{2,1,0:T(8,128)}, f32[2,256,256]{2,1,0:T(8,128)}) fusion(f32[2,12,256]{2,1,0:T(8,128)} %copy.878, f32[2,256,256]{2,1,0:T(8,128)} %fusion.311, f32[2,12,256]{2,1,0:T(8,128)} %copy.879, pred[2,256,256]{2,1,0:T(8,128)(4,1)} %compare_and_fusion.5, ...), kind=kOutput, calls=%fused_computation.111.clone.1 | convolution fusion | flops 1237694464 | bytes 4448256 | tf_op jit(solution)/shard_map/transpose(jvp(vmap()))/while/body/eval_jaxpr/checkpoint/hij,jhp->ihp/dot_general | solution.py:54
  396.2 6.3 reduce-window.74
  418.4 6.7 bitcast_dynamic-update-slice_fusion.42
  477.0 13.0 %fusion.312 = (f32[2,12,256]{2,1,0:T(8,128)}, f32[2,12,256]{2,1,0:T(8,128)}, f32[2,12,256]{2,1,0:T(8,128)}, f32[2,256,256]{2,1,0:T(8,128)}) fusion(f32[2,12,256]{2,1,0:T(8,128)} %copy.878, f32[2,256,256]{2,1,0:T(8,128)} %fusion.311, f32[2,12,256]{2,1,0:T(8,128)} %copy.879, pred[2,256,256]{2,1,0:T(8,128)(4,1)} %compare_and_fusion.5, ...), kind=kOutput, calls=%fused_computation.111.clone.1 | convolution fusion | flops 1237694464 | bytes 4448256 | tf_op jit(solution)/shard_map/transpose(jvp(vmap()))/while/body/eval_jaxpr/checkpoint/hij,jhp->ihp/dot_general | solution.py:54
  505.1 6.3 reduce-window.74
  527.3 6.7 bitcast_dynamic-update-slice_fusion.42
  563.4 10.5 %multiply_reduce_fusion.8 = (f32[768]{0:T(1024)S(1)}, f32[768]{0:T(1024)S(1)}, f32[768]{0:T(1024)S(1)}, f32[768]{0:T(1024)S(1)}, f32[768]{0:T(1024)S(1)}, /*index=5*/f32[2,512,768]{2,1,0:T(8,128)}) fusion(f32[2,512,768]{2,1,0:T(8,128)} %copy-done.19, f32[2,512]{1,0:T(2,128)S(1)} %copy-done.78, f32[2,512]{1,0:T(2,128)S(1)} %copy-done.80, ...), kind=kLoop, calls=%fused_computation.197 | loop fusion | flops 18084096 | bytes 15759360 | tf_op jit(solution)/shard_map/transpose(jvp(vmap()))/reduce_sum | solution.py:28
  631.2 6.1 fusion.122
  685.5 11.6 %collective-permute-start.43 = (bf16[512,1536]{1,0:T(8,128)(2,1)}, bf16[512,1536]{1,0:T(8,128)(2,1)}, u32[]{:S(2)}, u32[]{:S(2)}) collective-permute-start(bf16[512,1536]{1,0:T(8,128)(2,1)} %dynamic-slice_bitcast_fusion.5), channel_id=1, source_target_pairs={{0,2},{2,0},{1,3},{3,1},{4,6},{6,4},{5,7},{7,5},{8,10},{10,8},{9,1... | collective-permute-start | bytes 4718600 | tf_op jit(solution)/shard_map/ppermute | solution.py:96
  748.1 31.5 %collective-permute-done.73 = f32[12]{0:T(128)S(1)} collective-permute-done((f32[12]{0:T(128)S(1)}, f32[12]{0:T(128)S(1)}, u32[]{:S(2)}, u32[]{:S(2)}) %collective-permute-start.73) | collective-permute-done | bytes 80 | tf_op jit(solution)/shard_map/ppermute | solution.py:96
  (937 shorter events, 566.5 us)
Async XLA Ops:
  1.4 26.4 %collective-permute-start.2 = (bf16[24,768]{1,0:T(8,128)(2,1)S(1)}, bf16[24,768]{1,0:T(8,128)(2,1)S(1)}, u32[]{:S(2)}, u32[]{:S(2)}) collective-permute-start(bf16[24,768]{1,0:T(8,128)(2,1)S(1)} %constant_dynamic-slice_fusion.31), channel_id=1, source_target_pairs={{0,2},{2,0},{1,3},{3,1},{4,6},{6,4},{5,7},{7,5},{8,10},{10,8},{9,1... | collective-permute-start | bytes 110600 | tf_op jit(solution)/shard_map/ppermute | solution.py:96
  3.6 22.0 %collective-permute-start.3 = (bf16[12,256]{1,0:T(8,128)(2,1)}, bf16[12,256]{1,0:T(8,128)(2,1)S(1)}, u32[]{:S(2)}, u32[]{:S(2)}) collective-permute-start(bf16[12,256]{1,0:T(8,128)(2,1)} %param.27), channel_id=1, source_target_pairs={{0,1},{1,0},{2,3},{3,2},{4,5},{5,4},{6,7},{7,6},{8,9},{9,8},{10,11... | collective-permute-start | bytes 18440 | tf_op jit(solution)/shard_map/ppermute | solution.py:96
  5.1 111.2 %collective-permute-start = (bf16[256,1536]{1,0:T(8,128)(2,1)}, bf16[256,1536]{1,0:T(8,128)(2,1)S(1)}, u32[]{:S(2)}, u32[]{:S(2)}) collective-permute-start(bf16[256,1536]{1,0:T(8,128)(2,1)} %param.21), channel_id=1, source_target_pairs={{0,1},{1,0},{2,3},{3,2},{4,5},{5,4},{6,7},{7,6},{8,9},{9,8},{10,11... | collective-permute-start | bytes 2359304 | tf_op jit(solution)/shard_map/ppermute | solution.py:96
  22.5 102.1 %collective-permute-start.31 = (bf16[256,1536]{1,0:T(8,128)(2,1)}, bf16[256,1536]{1,0:T(8,128)(2,1)}, u32[]{:S(2)}, u32[]{:S(2)}) collective-permute-start(bf16[256,1536]{1,0:T(8,128)(2,1)} %param.22), channel_id=1, source_target_pairs={{0,1},{1,0},{2,3},{3,2},{4,5},{5,4},{6,7},{7,6},{8,9},{9,8},{10,11... | collective-permute-start | bytes 2359304 | tf_op jit(solution)/shard_map/ppermute | solution.py:96
  95.0 35.9 %collective-permute-start.28 = (bf16[2,4,48,768]{3,2,1,0:T(8,128)(2,1)}, bf16[2,4,48,768]{3,2,1,0:T(8,128)(2,1)}, u32[]{:S(2)}, u32[]{:S(2)}) collective-permute-start(bf16[2,4,48,768]{3,2,1,0:T(8,128)(2,1)} %bitcast_dynamic-update-slice_fusion.20), channel_id=1, source_target_pairs={{0,32},{32,64},{64,96},{96,0},{1,33},{33,65},{65,97},{97,1},{2,34}... | collective-permute-start | bytes 1769480 | tf_op jit(solution)/shard_map/ppermute | solution.py:100
  100.9 31.9 %collective-permute-start.29 = (bf16[2,4,48,768]{3,2,1,0:T(8,128)(2,1)}, bf16[2,4,48,768]{3,2,1,0:T(8,128)(2,1)}, u32[]{:S(2)}, u32[]{:S(2)}) collective-permute-start(bf16[2,4,48,768]{3,2,1,0:T(8,128)(2,1)} %bitcast_dynamic-update-slice_fusion.20), channel_id=1, source_target_pairs={{0,64},{32,96},{64,0},{96,32},{1,65},{33,97},{65,1},{97,33},{2,66}... | collective-permute-start | bytes 1769480 | tf_op jit(solution)/shard_map/ppermute | solution.py:100
  113.6 23.9 %collective-permute-start.30 = (bf16[2,4,48,768]{3,2,1,0:T(8,128)(2,1)}, bf16[2,4,48,768]{3,2,1,0:T(8,128)(2,1)}, u32[]{:S(2)}, u32[]{:S(2)}) collective-permute-start(bf16[2,4,48,768]{3,2,1,0:T(8,128)(2,1)} %bitcast_dynamic-update-slice_fusion.20), channel_id=1, source_target_pairs={{0,96},{32,0},{64,32},{96,64},{1,97},{33,1},{65,33},{97,65},{2,98}... | collective-permute-start | bytes 1769480 | tf_op jit(solution)/shard_map/ppermute | solution.py:100
  120.3 41.3 %collective-permute-start.1 = (bf16[512,1536]{0,1:T(8,128)(2,1)}, bf16[512,1536]{0,1:T(8,128)(2,1)}, u32[]{:S(2)}, u32[]{:S(2)}) collective-permute-start(bf16[512,1536]{0,1:T(8,128)(2,1)} %copy.763), channel_id=1, source_target_pairs={{0,2},{2,0},{1,3},{3,1},{4,6},{6,4},{5,7},{7,5},{8,10},{10,8},{9,1... | collective-permute-start | bytes 4718600 | tf_op jit(solution)/shard_map/ppermute | solution.py:96
  129.8 31.8 %collective-permute-start.32 = (bf16[512,1536]{0,1:T(8,128)(2,1)}, bf16[512,1536]{0,1:T(8,128)(2,1)S(1)}, u32[]{:S(2)}, u32[]{:S(2)}) collective-permute-start(bf16[512,1536]{0,1:T(8,128)(2,1)} %copy.766), channel_id=1, source_target_pairs={{0,2},{2,0},{1,3},{3,1},{4,6},{6,4},{5,7},{7,5},{8,10},{10,8},{9,1... | collective-permute-start | bytes 4718600 | tf_op jit(solution)/shard_map/ppermute | solution.py:96
  132.8 26.4 %collective-permute-start.39 = (bf16[4,2,48,768]{3,2,1,0:T(8,128)(2,1)S(1)}, bf16[4,2,48,768]{3,2,1,0:T(8,128)(2,1)S(1)}, u32[]{:S(2)}, u32[]{:S(2)}) collective-permute-start(bf16[4,2,48,768]{3,2,1,0:T(8,128)(2,1)S(1)} %copy-done.51), channel_id=1, source_target_pairs={{0,8},{4,12},{8,0},{12,4},{1,9},{5,13},{9,1},{13,5},{2,10},{6,14},... | collective-permute-start | bytes 1769480 | tf_op jit(solution)/shard_map/ppermute | solution.py:100
  137.6 24.0 %collective-permute-start.40 = (bf16[4,2,48,768]{3,2,1,0:T(8,128)(2,1)S(1)}, bf16[4,2,48,768]{3,2,1,0:T(8,128)(2,1)S(1)}, u32[]{:S(2)}, u32[]{:S(2)}) collective-permute-start(bf16[4,2,48,768]{3,2,1,0:T(8,128)(2,1)S(1)} %copy-done.51), channel_id=1, source_target_pairs={{0,12},{4,0},{8,4},{12,8},{1,13},{5,1},{9,5},{13,9},{2,14},{6,2},{... | collective-permute-start | bytes 1769480 | tf_op jit(solution)/shard_map/ppermute | solution.py:100
  299.5 352.8 %collective-permute-start.86 = (bf16[4,2,48,768]{3,2,1,0:T(8,128)(2,1)}, bf16[4,2,48,768]{3,2,1,0:T(8,128)(2,1)}, u32[]{:S(2)}, u32[]{:S(2)}) collective-permute-start(bf16[4,2,48,768]{3,2,1,0:T(8,128)(2,1)} %get-tuple-element.910), channel_id=1, source_target_pairs={{0,4},{4,8},{8,12},{12,0},{1,5},{5,9},{9,13},{13,1},{2,6},{6,10},{... | collective-permute-start | bytes 1769480 | tf_op jit(solution)/shard_map/ppermute | solution.py:100
  299.5 354.0 %collective-permute-start.87 = (bf16[4,2,48,768]{3,2,1,0:T(8,128)(2,1)}, bf16[4,2,48,768]{3,2,1,0:T(8,128)(2,1)}, u32[]{:S(2)}, u32[]{:S(2)}) collective-permute-start(bf16[4,2,48,768]{3,2,1,0:T(8,128)(2,1)} %get-tuple-element.912), channel_id=1, source_target_pairs={{0,8},{4,12},{8,0},{12,4},{1,9},{5,13},{9,1},{13,5},{2,10},{6,14},... | collective-permute-start | bytes 1769480 | tf_op jit(solution)/shard_map/ppermute | solution.py:100
  616.7 27.9 %collective-permute-start.49 = (bf16[2,4,48,768]{3,2,0,1:T(8,128)(2,1)}, bf16[2,4,48,768]{3,2,0,1:T(8,128)(2,1)}, u32[]{:S(2)}, u32[]{:S(2)}) collective-permute-start(bf16[2,4,48,768]{3,2,0,1:T(8,128)(2,1)} %bitcast.612), channel_id=1, source_target_pairs={{0,32},{32,64},{64,96},{96,0},{1,33},{33,65},{65,97},{97,1},{2,34}... | collective-permute-start | bytes 1769480 | tf_op jit(solution)/shard_map/ppermute | solution.py:100
  618.8 30.7 %collective-permute-start.50 = (bf16[2,4,48,768]{3,2,0,1:T(8,128)(2,1)}, bf16[2,4,48,768]{3,2,0,1:T(8,128)(2,1)}, u32[]{:S(2)}, u32[]{:S(2)}) collective-permute-start(bf16[2,4,48,768]{3,2,0,1:T(8,128)(2,1)} %bitcast.799), channel_id=1, source_target_pairs={{0,64},{32,96},{64,0},{96,32},{1,65},{33,97},{65,1},{97,33},{2,66}... | collective-permute-start | bytes 1769480 | tf_op jit(solution)/shard_map/ppermute | solution.py:100
  649.5 51.2 %collective-permute-start.57 = (bf16[4,2,48,512]{3,2,1,0:T(8,128)(2,1)S(1)}, bf16[4,2,48,512]{3,2,1,0:T(8,128)(2,1)S(1)}, u32[]{:S(2)}, u32[]{:S(2)}) collective-permute-start(bf16[4,2,48,512]{3,2,1,0:T(8,128)(2,1)S(1)} %get-tuple-element.917), channel_id=1, source_target_pairs={{0,4},{4,8},{8,12},{12,0},{1,5},{5,9},{9,13},{13,1},{2,6},{6,10},{... | collective-permute-start | bytes 1179656 | tf_op jit(solution)/shard_map/ppermute | solution.py:100
  649.5 53.0 %collective-permute-start.58 = (bf16[4,2,48,512]{3,2,1,0:T(8,128)(2,1)S(1)}, bf16[4,2,48,512]{3,2,1,0:T(8,128)(2,1)S(1)}, u32[]{:S(2)}, u32[]{:S(2)}) collective-permute-start(bf16[4,2,48,512]{3,2,1,0:T(8,128)(2,1)S(1)} %get-tuple-element.919), channel_id=1, source_target_pairs={{0,8},{4,12},{8,0},{12,4},{1,9},{5,13},{9,1},{13,5},{2,10},{6,14},... | collective-permute-start | bytes 1179656 | tf_op jit(solution)/shard_map/ppermute | solution.py:100
  677.0 26.8 %collective-permute-start.59 = (bf16[4,2,48,512]{3,2,1,0:T(8,128)(2,1)S(1)}, bf16[4,2,48,512]{3,2,1,0:T(8,128)(2,1)S(1)}, u32[]{:S(2)}, u32[]{:S(2)}) collective-permute-start(bf16[4,2,48,512]{3,2,1,0:T(8,128)(2,1)S(1)} %get-tuple-element.918), channel_id=1, source_target_pairs={{0,12},{4,0},{8,4},{12,8},{1,13},{5,1},{9,5},{13,9},{2,14},{6,2},{... | collective-permute-start | bytes 1179656 | tf_op jit(solution)/shard_map/ppermute | solution.py:100
  685.5 59.2 %collective-permute-start.43 = (bf16[512,1536]{1,0:T(8,128)(2,1)}, bf16[512,1536]{1,0:T(8,128)(2,1)}, u32[]{:S(2)}, u32[]{:S(2)}) collective-permute-start(bf16[512,1536]{1,0:T(8,128)(2,1)} %dynamic-slice_bitcast_fusion.5), channel_id=1, source_target_pairs={{0,2},{2,0},{1,3},{3,1},{4,6},{6,4},{5,7},{7,5},{8,10},{10,8},{9,1... | collective-permute-start | bytes 4718600 | tf_op jit(solution)/shard_map/ppermute | solution.py:96
  697.1 44.9 %collective-permute-start.47 = (bf16[512,1536]{1,0:T(8,128)(2,1)}, bf16[512,1536]{1,0:T(8,128)(2,1)}, u32[]{:S(2)}, u32[]{:S(2)}) collective-permute-start(bf16[512,1536]{1,0:T(8,128)(2,1)} %dynamic-slice_bitcast_fusion.4), channel_id=1, source_target_pairs={{0,2},{2,0},{1,3},{3,1},{4,6},{6,4},{5,7},{7,5},{8,10},{10,8},{9,1... | collective-permute-start | bytes 4718600 | tf_op jit(solution)/shard_map/ppermute | solution.py:96
  700.8 21.7 %collective-permute-start.92 = (bf16[48,768]{1,0:T(8,128)(2,1)}, bf16[48,768]{1,0:T(8,128)(2,1)}, u32[]{:S(2)}, u32[]{:S(2)}) collective-permute-start(bf16[48,768]{1,0:T(8,128)(2,1)} %dynamic-slice_bitcast_fusion.21), channel_id=1, source_target_pairs={{0,16},{16,0},{1,17},{17,1},{2,18},{18,2},{3,19},{19,3},{4,20},{20... | collective-permute-start | bytes 221192 | tf_op jit(solution)/shard_map/ppermute | solution.py:96
  743.9 36.3 %collective-permute-start.48 = (bf16[256,1536]{1,0:T(8,128)(2,1)S(1)}, bf16[256,1536]{1,0:T(8,128)(2,1)S(1)}, u32[]{:S(2)}, u32[]{:S(2)}) collective-permute-start(bf16[256,1536]{1,0:T(8,128)(2,1)S(1)} %constant_dynamic-slice_fusion.23), channel_id=1, source_target_pairs={{0,1},{1,0},{2,3},{3,2},{4,5},{5,4},{6,7},{7,6},{8,9},{9,8},{10,11... | collective-permute-start | bytes 2359304 | tf_op jit(solution)/shard_map/ppermute | solution.py:96
  746.5 34.3 %collective-permute-start.44 = (bf16[256,1536]{1,0:T(8,128)(2,1)S(1)}, bf16[256,1536]{1,0:T(8,128)(2,1)S(1)}, u32[]{:S(2)}, u32[]{:S(2)}) collective-permute-start(bf16[256,1536]{1,0:T(8,128)(2,1)S(1)} %constant_dynamic-slice_fusion.27), channel_id=1, source_target_pairs={{0,1},{1,0},{2,3},{3,2},{4,5},{5,4},{6,7},{7,6},{8,9},{9,8},{10,11... | collective-permute-start | bytes 2359304 | tf_op jit(solution)/shard_map/ppermute | solution.py:96
  747.5 32.1 %collective-permute-start.73 = (f32[12]{0:T(128)S(1)}, f32[12]{0:T(128)S(1)}, u32[]{:S(2)}, u32[]{:S(2)}) collective-permute-start(f32[12]{0:T(128)S(1)} %dynamic_slice.410), channel_id=1, source_target_pairs={{0,1},{1,0},{2,3},{3,2},{4,5},{5,4},{6,7},{7,6},{8,9},{9,8},{10,11... | collective-permute-start | bytes 152 | tf_op jit(solution)/shard_map/ppermute | solution.py:96
  (217 other events, 2742.7 us)
